TPU v7x, 32 devices: a whole 2x2x4 slice. The times are simulated.
32 devices in a mesh: pair: 2 (over x), grp: 2 (over core), proc: 8 (over z, y).
Axes of the slice: x: 2, y: 2, z: 4, core: 2. Of those that a mesh axis runs over, the one named last changes fastest.
Arguments:
- child_factor: bfloat16 [2, 24, 8, 128, 4096], P('pair', 'grp', 'proc'), parts along dimension 1, may hold values from -0.044194174 to 0.044194174
- child_update: float32 [2, 24, 8, 128, 1024], P('pair', 'grp', 'proc'), parts along dimension 1, may hold values from -0.2 to 0.2
- child_map: int32 [2, 192], P(None, 'grp'), parts along dimension 1, may hold values from 0 to 191, as said below
- parent_entries: float32 [48, 8, 128, 4, 2, 128], P('grp', 'proc', None, None, 'pair'), parts along dimension 0, may hold values from -0.3 to 10.3, as said below
Outputs:
- parent_factor: float32 [48, 8, 128, 4, 2, 128], P('grp', 'proc', None, None, 'pair'), parts along dimension 0
There are 2 independent parts, one for each index of `grp`. A program takes and returns all parts, laid end to end along the dimension named above; each array names one. Nothing has to cross between parts.
Inputs may be any that keep to these rules, and one draw needn't show every extreme that they name: `child_map`: for each child the map is one to one; the child row blocks held at [c, r, s] for one r go to parent row blocks q * 8 + d with one q and every d once; each child maps exactly 8 row blocks onto parent blocks 0 to 7; one device of a child sends at most 2 row blocks to parent blocks with one value of d, and reaches 2. `parent_entries`: off the diagonal entries are small; the diagonal is positive and dominant.
All inputs are finite; a program needn't handle non-finite values.
Results may differ from a plain program's by a relative error of at most 0.00095.
Values may be sent and summed in bfloat16 or wider, within the bound.
A program may use at most 128 MiB of HBM per device.

v0:
```python
import jax
import jax.numpy as jnp
from jax import lax
from jax.sharding import PartitionSpec as P

PANELS = 2


def from_root(shard, axis, root):
    mine = lax.axis_index(axis) == root
    return lax.psum(jnp.where(mine, shard, jnp.zeros_like(shard)), axis)


def shortened(shard):

    def short(part):
        return part.astype(jnp.bfloat16) if part.dtype == jnp.float32 else part

    return jax.tree.map(short, shard)


def send_table(block_map, proc_count, capacity):
    target = block_map % proc_count
    target_hit = (target[:, None] == jnp.arange(proc_count)[None, :]).astype(jnp.int32)
    slot_rank = jnp.cumsum(target_hit, axis=0) - 1
    slot_range = jnp.arange(capacity)
    return target_hit[:, :, None] * (slot_rank[:, :, None] == slot_range[None, None, :]).astype(
        jnp.int32
    )


def slot_table(all_maps, proc_count, my_proc, capacity):
    target = all_maps % proc_count
    local_block = all_maps // proc_count
    target_hit = (target == my_proc).astype(jnp.int32)
    slot_rank = jnp.cumsum(target_hit, axis=1) - 1
    slot_range = jnp.arange(capacity)
    matched = target_hit[..., None] * (slot_rank[..., None] == slot_range).astype(jnp.int32)
    return jnp.sum(matched * (local_block[..., None] + 1), axis=1) - 1


def body(child_factor, child_update, child_map, parent_entries):
    proc_count = lax.axis_size("proc")
    pair_count = lax.axis_size("pair")
    my_proc = lax.axis_index("proc")
    my_pair = lax.axis_index("pair")
    factor = child_factor[0, :, 0]
    update = child_update[0, :, 0]
    local_count = factor.shape[0]
    pivots = factor.shape[2]
    window_cols = update.shape[2]
    block_cols = window_cols // 128
    col_local = block_cols // 2
    capacity = -(-local_count // proc_count)
    all_maps = child_map.reshape(pair_count, local_count, proc_count)
    own_blocks = lax.dynamic_index_in_dim(
        lax.dynamic_index_in_dim(all_maps, my_pair, 0, False), my_proc, 1, False
    )
    factor_rows = factor.reshape(local_count * 128, pivots)
    slots_per = -(-block_cols // proc_count)
    inside = (all_maps < block_cols).astype(jnp.int32)
    seat_rank = jnp.cumsum(inside, axis=1) - 1
    seat_hit = inside[..., None] * (seat_rank[..., None] == jnp.arange(slots_per)).astype(jnp.int32)
    seat_ids = jnp.sum(seat_hit * (all_maps[..., None] + 1), axis=1) - 1
    own_ids = lax.dynamic_index_in_dim(seat_ids, my_pair, 0, False).reshape(proc_count * slots_per)
    own_hit = lax.dynamic_index_in_dim(
        lax.dynamic_index_in_dim(seat_hit, my_pair, 0, False), my_proc, 1, False
    )
    picked = jnp.einsum(
        "rc,rbk->cbk", own_hit.astype(jnp.bfloat16), factor, preferred_element_type=jnp.float32
    ).astype(jnp.bfloat16)
    partial_value = jnp.einsum(
        "rk,mbk->rmb",
        factor_rows,
        lax.all_gather(picked, "proc", axis=0, tiled=True),
        preferred_element_type=jnp.float32,
    )
    placer = (own_ids[:, None] == jnp.arange(block_cols)[None, :]).astype(jnp.float32)
    moved = jnp.einsum("rmb,mw->rwb", partial_value, placer, precision=lax.Precision.HIGHEST)
    product = moved.reshape(local_count * 128, window_cols)
    contrib = update.reshape(local_count * 128, window_cols) - product
    send_hit = send_table(own_blocks, proc_count, capacity).astype(jnp.float32)
    pieces = contrib.reshape(local_count, 128, col_local, pair_count, 128)
    packed = jnp.einsum("rdc,rahpe->pdcahe", send_hit, pieces, precision=lax.Precision.HIGHEST)
    moved_rows = lax.all_to_all(
        packed.reshape(pair_count * proc_count, capacity, 128, col_local, 128),
        ("pair", "proc"),
        split_axis=0,
        concat_axis=0,
        tiled=True,
    )
    arrived = moved_rows.reshape(pair_count * proc_count * capacity, 128 * col_local * 128)
    arrive_ids = slot_table(all_maps, proc_count, my_proc, capacity).reshape(
        pair_count * proc_count * capacity
    )
    local_rows = parent_entries.shape[0]
    onehot = (jnp.arange(local_rows)[:, None] == arrive_ids[None, :]).astype(jnp.float32)
    entries = parent_entries[:, 0, :, :, 0, :]
    matrix = entries + jnp.einsum(
        "qm,mx->qx", onehot, arrived, precision=lax.Precision.HIGHEST
    ).reshape(local_rows, 128, col_local, 128)
    rows_global = jnp.arange(local_rows) * proc_count + my_proc
    cols_global = jnp.arange(col_local) * 2 + my_pair
    lead_rows = -(-block_cols // proc_count)
    for panel_idx in range(PANELS):
        diag_local = panel_idx // proc_count
        diag_proc = panel_idx % proc_count
        diag_pair = panel_idx % 2
        diag_col = panel_idx // 2
        diag_block = from_root(matrix[diag_local, :, diag_col, :], "proc", diag_proc)
        pivot_factor = jnp.linalg.cholesky(jnp.tril(diag_block) + jnp.tril(diag_block, -1).T)
        column = matrix[:, :, diag_col, :].reshape(local_rows * 128, 128)
        solved = lax.linalg.triangular_solve(
            pivot_factor, column, left_side=False, lower=True, transpose_a=True
        ).reshape(local_rows, 128, 128)
        under_diag = (rows_global > panel_idx)[:, None, None]
        on_diag = (rows_global == panel_idx)[:, None, None]
        panel_rows = jnp.where(
            under_diag, solved, jnp.where(on_diag, pivot_factor[None], jnp.zeros_like(solved))
        )
        panel_rows = from_root(panel_rows, "pair", diag_pair)
        lead_block = lax.all_gather(
            shortened(panel_rows[:lead_rows][:, None]), "proc", axis=1, tiled=True
        ).reshape(lead_rows * proc_count, 128, 128)[:block_cols]
        mine_cols = lax.dynamic_index_in_dim(
            lead_block.reshape(col_local, 2, 128, 128), my_pair, 1, False
        )
        change = jnp.einsum("qax,hbx->qahb", panel_rows, mine_cols, precision=lax.Precision.HIGHEST)
        trailing = (cols_global > panel_idx)[None, None, :, None]
        is_panel = (cols_global == panel_idx)[None, None, :, None]
        matrix = jnp.where(
            is_panel,
            panel_rows[:, :, None, :],
            matrix - jnp.where(trailing, change, jnp.zeros_like(change)),
        )
    row_idx = rows_global[:, None] * 128 + jnp.arange(128)[None, :]
    col_idx = cols_global[:, None] * 128 + jnp.arange(128)[None, :]
    lower_part = row_idx[:, :, None, None] >= col_idx[None, None, :, :]
    result = jnp.where(lower_part, matrix, jnp.zeros_like(matrix))
    return result[:, None, :, :, None, :]


def solution(mesh):
    in_specs = (
        P("pair", "grp", "proc", None, None),
        P("pair", "grp", "proc", None, None),
        P(None, "grp"),
        P("grp", "proc", None, None, "pair", None),
    )
    out_specs = P("grp", "proc", None, None, "pair", None)
    return jax.shard_map(body, mesh=mesh, in_specs=in_specs, out_specs=out_specs, check_vma=False)
```

profile of v0, /device:TPU:0, one launch (start us, length us, event | category | flops | bytes accessed | tf_op | source)
XLA Modules:
  0.0 852.5 jit_solution(5915018736163681810)
XLA Ops:
  7.2 0.8 reshape.378
  8.8 19.6 %fusion = bf16[1,128,4096]{2,0,1:T(2,128)(2,1)S(1)} fusion(bf16[12,128,4096]{2,1,0:T(8,128)(2,1)} %bitcast.116, s32[1,12,1,1]{1,2,3,0:T(1,128)S(1)} %copy.186, pred[2,12,8,1]{1,2,3,0:T(8,128)(4,1)S(1)} %bitcast.125, s32[]{:T(128)S(6)} %select_n.145, s32[]{:T(128)S(6)} %select_n.147), kind=kOutput, calls=%fused_computation | convolution fusion | flops 12582936 | bytes 13632520 | tf_op jit(solution)/shard_map/rc,rbk->cbk/dot_general | solution.py:69
  28.5 2.1 copy.201
  30.6 6.6 copy.146
  37.2 6.8 copy.152
  44.4 114.0 %all-gather.5.cloned.1.call-done = bf16[1024,4096]{1,0:T(8,128)(2,1)} async-done(((bf16[128,4096]{1,0:T(8,128)(2,1)}), bf16[1024,4096]{1,0:T(8,128)(2,1)}) %all-gather.5.cloned.1.call-update) | async-done | bytes 8388624 | tf_op jit(solution)/shard_map/all_gather | solution.py:75
  158.4 19.6 %convolution_bitcast_fusion = f32[1536,8,128]{0,2,1:T(8,128)} fusion(bf16[8,128,4096]{2,1,0:T(8,128)(2,1)} %bitcast.126, bf16[1536,4096,1]{1,0,2:T(8,128)(2,1)} %bitcast.117), kind=kOutput, calls=%fused_computation.11 | convolution fusion | flops 12884901888 | bytes 27262976 | tf_op jit(solution)/shard_map/rk,mbk->rmb/dot_general | solution.py:72
  178.0 6.9 copy.150
  184.9 8.6 %fusion.43 = f32[8,1536,128]{2,0,1:T(8,128)} fusion(f32[1536,8,128]{2,1,0:T(8,128)} %copy.150, s32[8]{0:T(128)S(1)} %fusion.50), kind=kOutput, calls=%fused_computation.83 | convolution fusion | flops 150995008 | bytes 12582944 | tf_op jit(solution)/shard_map/rmb,mw->rwb/dot_general | solution.py:79
  193.5 4.5 fusion.6
  198.1 14.5 %fusion.7 = f32[2,8,2,128,4,128]{5,1,2,0,4,3:T(8,128)S(1)} fusion(f32[12,128,4,2,128,1]{4,1,3,2,0,5:T(8,128)S(1)} %fusion.6, s32[12,8]{0,1:T(8,128)S(1)} %fusion.45, s32[12,8]{0,1:T(8,128)S(1)} %broadcast_add_fusion.1), kind=kOutput, calls=%fused_computation.14 | convolution fusion | flops 301990464 | bytes 14680832 | tf_op jit(solution)/shard_map/rdc,rahpe->pdcahe/dot_general | solution.py:84
  212.6 8.1 copy.155
  220.7 4.7 all-to-all-start
  225.5 0.8 reduce_window_sum.28
  226.6 172.3 %all-to-all-done = f32[16,2,128,4,128]{4,2,3,1,0:T(8,128)} async-done(((f32[16,2,128,4,128]{4,2,3,1,0:T(8,128)}), f32[16,2,128,4,128]{4,2,3,1,0:T(8,128)}, u32[]{:S(2)}, u32[]{:S(2)}) %all-to-all-start) | async-done | bytes 8388640 | tf_op jit(solution)/shard_map/all_to_all | solution.py:85
  399.0 13.8 %copy.156 = f32[16,2,128,4,128]{4,3,2,1,0:T(4,128)} copy(f32[16,2,128,4,128]{4,2,3,1,0:T(8,128)} %all-to-all-done) | data formatting | bytes 16777216 | tf_op jit(solution)/shard_map/all_to_all | solution.py:85
  412.7 9.0 %reshape.381 = f32[32,65536]{1,0:T(8,128)} reshape(f32[16,2,128,4,128]{4,3,2,1,0:T(4,128)} %copy.156) | data formatting | bytes 16777216 | tf_op jit(solution)/shard_map/reshape | solution.py:92
  421.7 9.7 %dot_general.33 = f32[128,4,128,32]{2,1,0,3:T(4,128)} reshape(f32[65536,32]{0,1:T(8,128)} %bitcast.111) | data formatting | bytes 16777216 | tf_op jit(solution)/shard_map/qm,mx->qx/dot_general | solution.py:99
  431.5 11.6 %fusion.4 = f32[24,128,4,128]{3,0,2,1:T(8,128)S(1)} fusion(f32[128,4,128,32]{2,1,0,3:T(4,128)} %dot_general.33, s32[32]{0:T(128)S(1)} %sub.38), kind=kOutput, calls=%fused_computation.4 | convolution fusion | flops 603980544 | bytes 14680192 | tf_op jit(solution)/shard_map/qm,mx->qx/dot_general | solution.py:99
  443.1 6.6 bitcast_add_fusion
  449.7 2.7 copy-done.1
  453.3 1.5 slice.33
  454.8 74.6 %all-reduce.5.cloned.1.call-done = f32[128,128]{1,0:T(8,128)} async-done(((f32[128,128]{1,0:T(8,128)}), f32[128,128]{1,0:T(8,128)}) %all-reduce.5.cloned.1.call-update) | async-done | bytes 65552 | tf_op jit(solution)/shard_map/psum | solution.py:11
  529.4 0.9 copy.159
  530.3 0.9 bitcast_add_fusion.4
  531.4 11.7 %cholesky.44 = f32[128,128]{1,0:T(8,128)S(1)} custom-call(f32[128,128]{1,0:T(8,128)S(1)} %fusion.21), custom_call_target="Cholesky" | custom-call | tf_op jit(solution)/shard_map/jit(cholesky)/cholesky | solution.py:111
  543.1 0.7 compare_reduce_fusion.1
  544.5 9.8 %custom-call.6 = f32[1,128,128]{1,2,0:T(8,128)S(1)} custom-call(f32[1,128,128]{2,1,0:T(8,128)S(1)} %get-tuple-element.9), custom_call_target="InvertDiagBlocksLowerTriangular" | custom-call | tf_op jit(solution)/shard_map/triangular_solve/custom-call.0 | solution.py:113
  554.3 1.5 convolution_bitcast_fusion.2
  556.3 1.4 select_select_fusion.1
  558.0 51.4 %all-reduce.7.cloned.1.call-done = f32[24,128,128]{2,1,0:T(8,128)} async-done(((f32[24,128,128]{2,1,0:T(8,128)}), f32[24,128,128]{2,1,0:T(8,128)}) %all-reduce.7.cloned.1.call-update) | async-done | bytes 1572880 | tf_op jit(solution)/shard_map/psum | solution.py:11
  609.4 0.8 slice.47
  610.2 30.8 %all-gather.1 = bf16[8,128,128]{2,1,0:T(8,128)(2,1)S(1)} all-gather(bf16[1,128,128]{2,1,0:T(8,128)(2,1)S(1)} %slice.47), channel_id=3, replica_groups=mesh['pair'=2,'grp'=2,'proc'=8] {'proc'}, dimensions={0}, use_global_device_ids=true | all-gather | bytes 294912 | tf_op jit(solution)/shard_map/all_gather | solution.py:122
  641.0 7.3 subtract_select_fusion
  648.3 2.7 copy-done
  652.0 1.5 slice.36
  653.5 66.8 %all-reduce.9.cloned.1.call-done = f32[128,128]{1,0:T(8,128)} async-done(((f32[128,128]{1,0:T(8,128)}), f32[128,128]{1,0:T(8,128)}) %all-reduce.9.cloned.1.call-update) | async-done | bytes 65552 | tf_op jit(solution)/shard_map/psum | solution.py:11
  720.3 0.8 broadcast_select_fusion
  721.2 0.9 bitcast_add_fusion.2
  722.2 11.7 %cholesky.55 = f32[128,128]{1,0:T(8,128)S(1)} custom-call(f32[128,128]{1,0:T(8,128)S(1)} %fusion.19), custom_call_target="Cholesky" | custom-call | tf_op jit(solution)/shard_map/jit(cholesky)/cholesky | solution.py:111
  735.4 9.8 %custom-call.7 = f32[1,128,128]{1,2,0:T(8,128)S(1)} custom-call(f32[1,128,128]{2,1,0:T(8,128)S(1)} %get-tuple-element.6), custom_call_target="InvertDiagBlocksLowerTriangular" | custom-call | tf_op jit(solution)/shard_map/triangular_solve/custom-call.0 | solution.py:113
  745.2 1.5 convolution_bitcast_fusion.1
  747.2 1.4 select_select_fusion
  748.9 51.4 %all-reduce.11.cloned.1.call-done = f32[24,128,128]{2,1,0:T(8,128)} async-done(((f32[24,128,128]{2,1,0:T(8,128)}), f32[24,128,128]{2,1,0:T(8,128)}) %all-reduce.11.cloned.1.call-update) | async-done | bytes 1572880 | tf_op jit(solution)/shard_map/psum | solution.py:11
  800.3 0.8 slice.46
  801.1 30.8 %all-gather.2 = bf16[8,128,128]{2,1,0:T(8,128)(2,1)S(1)} all-gather(bf16[1,128,128]{2,1,0:T(8,128)(2,1)S(1)} %slice.46), channel_id=4, replica_groups=mesh['pair'=2,'grp'=2,'proc'=8] {'proc'}, dimensions={0}, use_global_device_ids=true | all-gather | bytes 294912 | tf_op jit(solution)/shard_map/all_gather | solution.py:122
  831.9 6.1 select_bitcast_fusion
  838.0 7.5 copy.169
  (62 shorter events, 7.9 us)
Async XLA Ops:
  6.5 151.9 %all-gather.5.cloned.1.call-start = ((), (), s32[]{:S(2)}) async-start(), calls=%async_computation.5 | async-start | bytes 9437184 | tf_op jit(solution)/shard_map/all_gather | solution.py:75
  178.0 15.6 %slice-start = ((s8[6291456]{0:T(1024)(128)(4,1)}), s8[2097152]{0:T(1024)(128)(4,1)S(1)}, s32[]{:S(2)}) async-start(s8[6291456]{0:T(1024)(128)(4,1)} %bitcast.113), calls=%async_computation.6 | async-start | bytes 4194304
  184.9 8.6 %slice-start.1 = ((s8[6291456]{0:T(1024)(128)(4,1)}), s8[4194304]{0:T(1024)(128)(4,1)S(1)}, s32[]{:S(2)}) async-start(s8[6291456]{0:T(1024)(128)(4,1)} %bitcast.113), calls=%async_computation.7 | async-start | bytes 8388608
  220.7 178.3 %all-to-all-start = ((f32[16,2,128,4,128]{4,2,3,1,0:T(8,128)}), f32[16,2,128,4,128]{4,2,3,1,0:T(8,128)}, u32[]{:S(2)}, u32[]{:S(2)}) async-start(f32[16,2,128,4,128]{4,2,3,1,0:T(8,128)} %bitcast.110), calls=%async_computation | async-start | bytes 16777216 | tf_op jit(solution)/shard_map/all_to_all | solution.py:85
  225.4 303.9 %all-reduce.5.cloned.1.call-start = ((), (), s32[]{:S(2)}) async-start(), calls=%async_computation.1 | async-start | bytes 131072 | tf_op jit(solution)/shard_map/psum | solution.py:11
  449.6 2.7 copy-start.1
  453.0 156.4 %all-reduce.7.cloned.1.call-start = ((), (), s32[]{:S(2)}) async-start(), calls=%async_computation.2 | async-start | bytes 3145728 | tf_op jit(solution)/shard_map/psum | solution.py:11
  557.8 162.5 %all-reduce.9.cloned.1.call-start = ((), (), s32[]{:S(2)}) async-start(), calls=%async_computation.3 | async-start | bytes 131072 | tf_op jit(solution)/shard_map/psum | solution.py:11
  648.3 2.7 copy-start
  651.7 148.6 %all-reduce.11.cloned.1.call-start = ((), (), s32[]{:S(2)}) async-start(), calls=%async_computation.4 | async-start | bytes 3145728 | tf_op jit(solution)/shard_map/psum | solution.py:11
Sparse Core Ops, SparseCore 0:
  30.7 127.6 all-gather.4
  453.1 76.1 all-reduce.4
  557.9 51.4 all-reduce.6
  651.8 68.4 all-reduce.8
  748.8 51.4 all-reduce.10
where the time goes:
time: 862 us; the launch traced here: 852 us
  waiting for transfers between devices  531 us (62%)
  matrix products  90.4 us (10%)
  local copies, waits for them, and re-layouts  84.3 us (10%)
  other arithmetic  66.4 us (8%)
  blocking collectives  61.6 us (7%)
  between operations  13.9 us (2%)
    psum x4, waiting for transfers between devices, from_root(): return lax.psum(jnp.where(mine, shard, jnp.zeros_like(shard)), axis)  244 us
    all_to_all x1, waiting for transfers between devices, body(): lax.all_to_all(packed.reshape(pair_count * proc_count, capacity, 128, col...  172 us
    all_gather x1, waiting for transfers between devices, body(): lax.all_gather(picked, 'proc', axis=0, tiled=True)  114 us
    all_gather x2, blocking collectives, body(): lax.all_gather(shortened(panel_rows[:lead_rows][:, None]), 'proc', axis=1...  61.6 us
    another operation x6, other arithmetic, body(): jnp.linalg.cholesky(jnp.tril(diag_block) + jnp.tril(diag_block, -1).T)  24.9 us
    another operation x4, other arithmetic, body(): lax.linalg.triangular_solve(pivot_factor, column, left_side=False, lower=...  21 us
    dot_general x1, matrix products, body(): jnp.einsum('rc,rbk->cbk', own_hit.astype(jnp.bfloat16), factor, preferred...  19.6 us
    dot_general x1, matrix products, body(): jnp.einsum('rk,mbk->rmb', factor_rows, lax.all_gather(picked, 'proc', axi...  19.6 us
  transfers between devices with their start and end apart: 6, of which 6 were waited for; matrix products, arithmetic and copies ran while one was open for 2% of the time, Pallas kernels for 0%

commit v1 on v0

v1 whole, which is shorter than its diff:
```python
import functools

import jax
import jax.numpy as jnp
from jax import lax
from jax.experimental import pallas as pl
from jax.experimental.pallas import tpu as pltpu
from jax.sharding import PartitionSpec as P

HIGHEST = lax.Precision.HIGHEST
NT = (((1,), (1,)), ((), ()))
LINK = jnp.float16
VMEM_LIMIT = 60 * 1024 * 1024


def nt_dot(a, b):
    return lax.dot_general(a, b, NT, precision=HIGHEST, preferred_element_type=jnp.float32)


def contrib_kernel(half, slots, seats, factor_ref, update_ref, *rest):
    window_refs, out_ref, window = rest[: 2 * half], rest[2 * half], rest[2 * half + 1]

    @pl.when(pl.program_id(0) == 0)
    def _():
        for p in range(2):
            for h in range(half):
                window[p, h * 128 : (h + 1) * 128, :] = window_refs[2 * h + p][0]

    for p in range(2):
        product = lax.dot_general(
            factor_ref[0], window[p], NT, preferred_element_type=jnp.float32
        )
        for h in range(half):
            w = 2 * h + p
            out_ref[p, 0, :, h * 128 : (h + 1) * 128] = (
                update_ref[0, :, w * 128 : (w + 1) * 128] - product[:, h * 128 : (h + 1) * 128]
            ).astype(out_ref.dtype)


def contrib_blocks(factor, update, gathered, slots, seats, slot_count):
    rows, _, pivots = factor.shape
    cols = update.shape[2]
    half = cols // 256

    def seat_map(w):
        return lambda i, slots, seats: (seats[w], 0, 0)

    return pl.pallas_call(
        functools.partial(contrib_kernel, half),
        out_shape=jax.ShapeDtypeStruct((2, slot_count, 128, half * 128), jnp.float32),
        grid_spec=pltpu.PrefetchScalarGridSpec(
            num_scalar_prefetch=2,
            grid=(rows,),
            in_specs=[
                pl.BlockSpec((1, 128, pivots), lambda i, slots, seats: (i, 0, 0)),
                pl.BlockSpec((1, 128, cols), lambda i, slots, seats: (i, 0, 0)),
            ]
            + [pl.BlockSpec((1, 128, pivots), seat_map(w)) for w in range(2 * half)],
            out_specs=pl.BlockSpec(
                (2, 1, 128, half * 128), lambda i, slots, seats: (0, slots[i], 0, 0)
            ),
            scratch_shapes=[pltpu.VMEM((2, half * 128, pivots), jnp.bfloat16)],
        ),
        compiler_params=pltpu.CompilerParams(vmem_limit_bytes=VMEM_LIMIT),
        name="contrib",
    )(slots, seats, factor, update, *([gathered] * (2 * half)))


def column_kernel(group, half, where, entries_ref, *rest):
    arrived, out_ref = rest[: 2 * group], rest[2 * group]
    step = pl.program_id(0)
    count = where.shape[0] // 2
    for g in range(group):
        value = entries_ref[g, pl.ds(0, 128, stride=half), :]
        for c in range(2):
            spot = where[c * count + step * group + g]
            part = arrived[2 * g + c][0].astype(jnp.float32)
            value = value + jnp.where(spot >= 0, part, 0.0)
        out_ref[g] = value


def arrived_specs(group, count, width):
    def spot(c, g):
        return lambda i, where, *more: (jnp.maximum(where[c * count + i * group + g], 0), 0, 0)

    return [pl.BlockSpec((1, 128, width), spot(c, g)) for g in range(group) for c in range(2)]


def raw_column(entries, arrived, where, group):
    count, rows, _ = entries.shape
    half = rows // 128
    return pl.pallas_call(
        functools.partial(column_kernel, group, half),
        out_shape=jax.ShapeDtypeStruct((count, 128, 128), jnp.float32),
        grid_spec=pltpu.PrefetchScalarGridSpec(
            num_scalar_prefetch=1,
            grid=(count // group,),
            in_specs=[pl.BlockSpec((group, rows, 128), lambda i, where: (i, 0, 0))]
            + arrived_specs(group, count, 128),
            out_specs=pl.BlockSpec((group, 128, 128), lambda i, where: (i, 0, 0)),
        ),
        compiler_params=pltpu.CompilerParams(vmem_limit_bytes=VMEM_LIMIT),
        name="raw_column",
    )(where, entries, *([arrived] * (2 * group)))


def finish_kernel(group, half, where, place, entries_ref, zero_ref, one_ref, small_ref, lead_ref, *rest):
    arrived, out_ref = rest[: 2 * group], rest[2 * group]
    step = pl.program_id(0)
    count = where.shape[0] // 2
    my_proc, my_pair, proc_count = place[0], place[1], place[2]
    rows = group * 128
    block = (step * group + lax.broadcasted_iota(jnp.int32, (rows, 1), 0) // 128) * proc_count + my_proc

    def spread(k):
        return jnp.broadcast_to(small_ref[k][None], (group, 128, 128)).reshape(rows, 128)

    first = nt_dot(zero_ref[...].reshape(rows, 128), small_ref[0])
    first = jnp.where(block > 0, first, spread(1))
    second = nt_dot(one_ref[...].reshape(rows, 128) - nt_dot(first, small_ref[4]), small_ref[2])
    second = jnp.where(block > 1, second, jnp.where(block == 1, spread(3), 0.0))
    change = nt_dot(jnp.concatenate([first, second], axis=1), lead_ref[128:, :])
    row_id = block * 128 + lax.broadcasted_iota(jnp.int32, (rows, 1), 0) % 128
    lane = lax.broadcasted_iota(jnp.int32, (1, 128), 1)
    panel = jnp.where(my_pair == 0, first, second)
    for h in range(half):
        lower = row_id >= (2 * h + my_pair) * 128 + lane
        for g in range(group):
            span = slice(g * 128, (g + 1) * 128)
            if h == 0:
                value = panel[span]
            else:
                value = entries_ref[g, pl.ds(h, 128, stride=half), :]
                for c in range(2):
                    spot = where[c * count + step * group + g]
                    part = arrived[2 * g + c][0, :, h * 128 : (h + 1) * 128].astype(jnp.float32)
                    value = value + jnp.where(spot >= 0, part, 0.0)
                value = value - change[span, (h - 1) * 128 : h * 128]
            out_ref[g, pl.ds(h, 128, stride=half), :] = jnp.where(lower[span], value, 0.0)


def finish(entries, arrived, where, place, zero, one, small, lead, group):
    count, rows, _ = entries.shape
    half = rows // 128
    by_row = lambda i, where, place: (i, 0, 0)
    return pl.pallas_call(
        functools.partial(finish_kernel, group, half),
        out_shape=jax.ShapeDtypeStruct(entries.shape, jnp.float32),
        grid_spec=pltpu.PrefetchScalarGridSpec(
            num_scalar_prefetch=2,
            grid=(count // group,),
            in_specs=[
                pl.BlockSpec((group, rows, 128), by_row),
                pl.BlockSpec((group, 128, 128), by_row),
                pl.BlockSpec((group, 128, 128), by_row),
                pl.BlockSpec(small.shape, lambda i, where, place: (0, 0, 0)),
                pl.BlockSpec(lead.shape, lambda i, where, place: (0, 0)),
            ]
            + arrived_specs(group, count, half * 128),
            out_specs=pl.BlockSpec((group, rows, 128), by_row),
        ),
        compiler_params=pltpu.CompilerParams(vmem_limit_bytes=VMEM_LIMIT),
        name="finish",
    )(where, place, entries, zero, one, small, lead, *([arrived] * (2 * group)))


def pivot_of(block):
    pivot = jnp.linalg.cholesky(jnp.tril(block) + jnp.tril(block, -1).T)
    inverse = lax.linalg.triangular_solve(
        pivot, jnp.eye(128, dtype=jnp.float32), left_side=True, lower=True
    )
    return pivot, inverse


def times_t(a, b):
    return jnp.einsum("qax,bx->qab", a, b, precision=HIGHEST)


def body(child_factor, child_update, child_map, parent_entries):
    proc_count = lax.axis_size("proc")
    pair_count = lax.axis_size("pair")
    my_proc = lax.axis_index("proc")
    my_pair = lax.axis_index("pair")
    _, local_count, _, _, pivots = child_factor.shape
    window_cols = child_update.shape[4]
    block_cols = window_cols // 128
    half = block_cols // 2
    capacity = -(-local_count // proc_count)
    slot_count = proc_count * capacity
    local_rows = parent_entries.shape[0]
    factor = child_factor.reshape(local_count, 128, pivots)
    update = child_update.reshape(local_count, 128, window_cols)
    entries = parent_entries.reshape(local_rows, 128 * half, 128)

    all_maps = child_map.reshape(pair_count, local_count, proc_count)
    child_maps = lax.dynamic_index_in_dim(all_maps, my_pair, 0, False)
    lead_at = jnp.argmax((child_maps < proc_count).astype(jnp.int32), axis=0)
    lead_ids = jnp.min(jnp.where(child_maps < proc_count, child_maps, proc_count), axis=0)
    seats = jnp.argmax(
        (lead_ids[None, :] == jnp.arange(block_cols)[:, None]).astype(jnp.int32), axis=1
    ).astype(jnp.int32)
    own_blocks = lax.dynamic_index_in_dim(child_maps, my_proc, 1, False)
    target = own_blocks % proc_count
    order = jnp.arange(local_count)
    rank = jnp.sum(
        ((target[:, None] == target[None, :]) & (order[None, :] < order[:, None])).astype(jnp.int32),
        axis=1,
    )
    slots = (target * capacity + rank).astype(jnp.int32)
    hit = all_maps % proc_count == my_proc
    hit_rank = jnp.cumsum(hit.astype(jnp.int32), axis=1) - 1
    source = (
        jnp.arange(pair_count)[:, None, None] * proc_count + jnp.arange(proc_count)[None, None, :]
    ) * capacity + hit_rank
    match = hit[..., None] & (all_maps[..., None] // proc_count == jnp.arange(local_rows))
    where = jnp.max(jnp.where(match, source[..., None], -1), axis=(1, 2))
    where = where.reshape(pair_count * local_rows).astype(jnp.int32)

    picked = lax.dynamic_index_in_dim(
        factor, lax.dynamic_index_in_dim(lead_at, my_proc, 0, False), 0, True
    )
    gathered = lax.all_gather(picked, "proc", axis=0, tiled=True)
    packed = contrib_blocks(factor, update, gathered, slots, seats, slot_count)
    arrived = lax.all_to_all(
        packed.astype(LINK).reshape(pair_count * proc_count, capacity, 128, half * 128),
        ("pair", "proc"),
        split_axis=0,
        concat_axis=0,
        tiled=True,
    ).reshape(pair_count * slot_count, 128, half * 128)
    arrived = arrived.astype(jnp.float32)

    column = raw_column(entries, arrived, where, 4)
    lead = lax.all_gather(column[0], ("pair", "proc"), axis=0, tiled=False)
    lead = lead.reshape(2, proc_count, 128, 128)
    other = lax.ppermute(column.astype(LINK), "pair", [(0, 1), (1, 0)]).astype(jnp.float32)
    other_lead = lax.dynamic_index_in_dim(
        lax.dynamic_index_in_dim(lead, 1 - my_pair, 0, False), my_proc, 0, True
    )
    other = jnp.concatenate([other_lead, other[1:]], axis=0)
    zero = jnp.where(my_pair == 0, column, other)
    one = jnp.where(my_pair == 0, other, column)

    ids = jnp.arange(block_cols)[:, None, None]
    pivot0, inverse0 = pivot_of(lead[0, 0])
    first = jnp.where(ids > 0, times_t(lead[0, :block_cols], inverse0), pivot0)
    rest = lead[1, :block_cols] - times_t(first, first[1])
    pivot1, inverse1 = pivot_of(rest[1])
    second = jnp.where(ids > 1, times_t(rest, inverse1), jnp.where(ids == 1, pivot1, 0.0))
    both = jnp.concatenate([first, second], axis=2)
    mine = lax.dynamic_index_in_dim(both.reshape(half, 2, 128, 256), my_pair, 1, False)
    small = jnp.stack([inverse0, pivot0, inverse1, pivot1, first[1]])
    place = jnp.stack([my_proc, my_pair, jnp.int32(proc_count)]).astype(jnp.int32)
    result = finish(
        entries, arrived, where, place, zero, one, small, mine.reshape(half * 128, 256), 4
    )
    return result.reshape(local_rows, 1, 128, half, 1, 128)


def solution(mesh):
    in_specs = (
        P("pair", "grp", "proc", None, None),
        P("pair", "grp", "proc", None, None),
        P(None, "grp"),
        P("grp", "proc", None, None, "pair", None),
    )
    out_specs = P("grp", "proc", None, None, "pair", None)
    return jax.shard_map(body, mesh=mesh, in_specs=in_specs, out_specs=out_specs, check_vma=False)
```

time: 862 us -> 452 us (0.52); the launches traced: 852 us -> 451 us
  waiting for transfers between devices: 531 us -> 267 us
  matrix products: 90.4 us -> 6.51 us
  local copies, waits for them, and re-layouts: 84.3 us -> 13.4 us
  Pallas kernels: 0 us -> 69.1 us
  blocking collectives: 61.6 us -> 0 us
    psum x4 -> x0, waiting for transfers between devices: 244 us -> none  [from_root(): return lax.psum(jnp.where(mine, shard, jnp.zeros_like(shard)), axis)]
    all_to_all x1, waiting for transfers between devices: 172 us -> 88.3 us  [body(): lax.all_to_all(packed.astype(LINK).reshape(pair_count * proc_count, capac...]
    dot_general x7 -> x3, matrix products: 87.4 us -> 5.1 us  [times_t(): return jnp.einsum('qax,bx->qab', a, b, precision=HIGHEST)]
    pallas_call x0 -> x3, Pallas kernels: none -> 69.1 us  [the longest x1 41.7 us: contrib_blocks(): pl.pallas_call(functools.partial(contrib_kernel, half), out_shape=jax.Sha...]
    all_gather x2 -> x0, blocking collectives: 61.6 us -> none  [body(): lax.all_gather(shortened(panel_rows[:lead_rows][:, None]), 'proc', axis=1...]
    all_gather x1 -> x2, waiting for transfers between devices: 114 us -> 164 us  [the longest x1 126 us: body(): gathered = lax.all_gather(picked, 'proc', axis=0, tiled=True)]
    dot_general x3 -> x0, local copies, waits for them, and re-layouts: 18.8 us -> none  [the longest x1 9.73 us: body(): jnp.einsum('qm,mx->qx', onehot, arrived, precision=lax.Precision.HIGHEST)]
    ppermute x0 -> x1, waiting for transfers between devices: none -> 14.5 us  [body(): lax.ppermute(column.astype(LINK), 'pair', [(0, 1), (1, 0)])]
  transfers between devices with their start and end apart: 6 -> 4, of which waited for: 6 -> 4; matrix products, arithmetic and copies ran while one was open for 2% -> 1% of each run, Pallas kernels for 0% -> 0%
where the time goes in v1:
time: 452 us; the launch traced here: 451 us
  waiting for transfers between devices  267 us (59%)
  other arithmetic  73.6 us (16%)
  Pallas kernels  69.1 us (15%)
  between operations  15.6 us (3%)
  local copies, waits for them, and re-layouts  13.4 us (3%)
  matrix products  6.51 us (1%)
  starting transfers between devices  6.18 us (1%)
    all_gather x1, waiting for transfers between devices, body(): gathered = lax.all_gather(picked, 'proc', axis=0, tiled=True)  126 us
    all_to_all x1, waiting for transfers between devices, body(): lax.all_to_all(packed.astype(LINK).reshape(pair_count * proc_count, capac...  88.3 us
    pallas_call x1, Pallas kernels, contrib_blocks(): pl.pallas_call(functools.partial(contrib_kernel, half), out_shape=jax.Sha...  41.7 us
    all_gather x1, waiting for transfers between devices, body(): lead = lax.all_gather(column[0], ('pair', 'proc'), axis=0, tiled=False)  38.3 us
    another operation x6, other arithmetic, pivot_of(): pivot = jnp.linalg.cholesky(jnp.tril(block) + jnp.tril(block, -1).T)  25.8 us
    another operation x4, other arithmetic, pivot_of(): lax.linalg.triangular_solve(pivot, jnp.eye(128, dtype=jnp.float32), left_...  23.7 us
    pallas_call x1, Pallas kernels, finish(): pl.pallas_call(functools.partial(finish_kernel, group, half), out_shape=j...  20.6 us
    ppermute x1, waiting for transfers between devices, body(): lax.ppermute(column.astype(LINK), 'pair', [(0, 1), (1, 0)])  14.5 us
  transfers between devices with their start and end apart: 4, of which 4 were waited for; matrix products, arithmetic and copies ran while one was open for 1% of the time, Pallas kernels for 0%

profile of v1, /device:TPU:0, one launch (start us, length us, event | category | flops | bytes accessed | tf_op | source)
XLA Modules:
  0.0 451.5 jit_solution(3449259424991986846)
XLA Ops:
  6.5 0.8 reshape.251
  7.4 0.6 fusion.23
  8.0 0.6 dynamic_slice.32
  10.5 2.3 constant_dynamic-slice_fusion.2
  13.4 0.6 multiply_add_fusion.slots
  13.9 0.7 iota_reduce_fusion
  14.6 126.1 %all-gather.6.cloned.1.call-done = bf16[8,1,1,128,4096]{4,3,2,1,0:T(8,128)(2,1)} async-done(((bf16[1,1,1,128,4096]{4,3,2,1,0:T(8,128)(2,1)}), bf16[8,1,1,128,4096]{4,3,2,1,0:T(8,128)(2,1)}) %all-gather.6.cloned.1.call-update) | async-done | bytes 8388624 | tf_op jit(solution)/shard_map/all_gather | solution.py:222
  140.7 41.7 %contrib.1 = f32[2,16,128,512]{3,2,1,0:T(8,128)} custom-call(s32[12]{0:T(128)} %multiply_add_fusion.slots, s32[8]{0:T(128)} %get-tuple-element.9.seats, bf16[12,128,4096]{2,1,0:T(8,128)(2,1)} %bitcast.91, f32[12,128,1024]{2,1,0:T(8,128)} %bitcast.92, bf16[8,128,4096]{2,1,0:T(8,128)(2,1)} %bitcast.80, bf16[8,128,4096]{2,1,0:T(8,128)(2,1)} %bitcast.81, ...), custom_call_target="tpu_custom_call" | custom-call | tf_op jit(solution)/shard_map/contrib/pallas_call | solution.py:48
  182.4 6.3 %convert_element_type.38 = f16[2,16,128,512]{3,2,1,0:T(8,128)(2,1)} convert(f32[2,16,128,512]{3,2,1,0:T(8,128)} %contrib.1) | non-fusion elementwise | flops 2097152 | bytes 12582912 | tf_op jit(solution)/shard_map/convert_element_type | solution.py:225
  188.6 4.6 %all-to-all-start = ((f16[16,2,128,512]{3,2,1,0:T(8,128)(2,1)}), f16[16,2,128,512]{3,2,1,0:T(8,128)(2,1)}, u32[]{:S(2)}, u32[]{:S(2)}) async-start(f16[16,2,128,512]{3,2,1,0:T(8,128)(2,1)} %bitcast.90), calls=%async_computation | async-start | bytes 8388608 | tf_op jit(solution)/shard_map/all_to_all | solution.py:224
  193.6 0.6 reshape.252.where
  194.2 88.3 %all-to-all-done = f16[16,2,128,512]{3,2,1,0:T(8,128)(2,1)} async-done(((f16[16,2,128,512]{3,2,1,0:T(8,128)(2,1)}), f16[16,2,128,512]{3,2,1,0:T(8,128)(2,1)}, u32[]{:S(2)}, u32[]{:S(2)}) %all-to-all-start) | async-done | bytes 4194336 | tf_op jit(solution)/shard_map/all_to_all | solution.py:224
  282.5 6.5 %bitcast_convert_fusion.rest_0_.rest_1_.rest_2_.rest_3_.rest_4_.rest_5_.rest_6_.rest_7_ = f32[32,128,512]{2,1,0:T(8,128)} fusion(f16[16,2,128,512]{3,2,1,0:T(8,128)(2,1)} %all-to-all-done), kind=kLoop, calls=%fused_computation | loop fusion | flops 2097152 | bytes 12582912 | tf_op jit(solution)/shard_map/convert_element_type | solution.py:231
  289.0 6.8 %raw_column.1 = f32[24,128,128]{2,1,0:T(8,128)} custom-call(s32[48]{0:T(128)} %reshape.252.where, f32[24,512,128]{2,1,0:T(8,128)} %bitcast.88, f32[32,128,512]{2,1,0:T(8,128)} %bitcast_convert_fusion.rest_0_.rest_1_.rest_2_.rest_3_.rest_4_.rest_5_.rest_6_.rest_7_, ...), custom_call_target="tpu_custom_call" | custom-call | tf_op jit(solution)/shard_map/raw_column/pallas_call | solution.py:92
  295.8 1.5 slice.41
  297.2 1.6 convert_element_type.41
  298.8 1.6 collective-permute-start
  300.5 0.5 iota_compare_fusion.10
  301.1 0.7 pad_add_fusion.place
  301.7 0.5 iota_compare_fusion.8
  302.2 14.5 %collective-permute-done = f16[24,128,128]{2,1,0:T(8,128)(2,1)S(1)} collective-permute-done((f16[24,128,128]{2,1,0:T(8,128)(2,1)S(1)}, f16[24,128,128]{2,1,0:T(8,128)(2,1)S(1)}, u32[]{:S(2)}, u32[]{:S(2)}) %collective-permute-start) | collective-permute-done | bytes 786464 | tf_op jit(solution)/shard_map/ppermute | solution.py:236
  316.8 38.3 %all-gather.4.cloned.1.call-done = f32[16,128,128]{2,1,0:T(8,128)} async-done(((f32[1,128,128]{2,1,0:T(8,128)}), f32[16,128,128]{2,1,0:T(8,128)}) %all-gather.4.cloned.1.call-update) | async-done | bytes 1048592 | tf_op jit(solution)/shard_map/all_gather | solution.py:234
  355.1 1.6 copy.64
  357.0 11.7 %cholesky.44 = f32[128,128]{1,0:T(8,128)S(1)} custom-call(f32[128,128]{1,0:T(8,128)S(1)} %copy.69), custom_call_target="Cholesky" | custom-call | tf_op jit(solution)/shard_map/jit(cholesky)/cholesky | solution.py:168
  368.8 0.6 compare_reduce_fusion.1
  369.4 0.6 select_bitcast_fusion.1
  370.1 9.8 %custom-call.6 = f32[1,128,128]{1,2,0:T(8,128)S(1)} custom-call(f32[1,128,128]{2,1,0:T(8,128)S(1)} %get-tuple-element.13), custom_call_target="InvertDiagBlocksLowerTriangular" | custom-call | tf_op jit(solution)/shard_map/triangular_solve/custom-call.0 | solution.py:169
  380.0 0.3 bitcast_dynamic-update-slice_fusion.3
  380.3 1.7 convolution_select_fusion
  382.0 0.8 copy-done.1
  382.8 1.6 convolution_subtract_fusion
  384.5 0.8 copy-done.2
  385.3 0.7 copy.72
  386.0 0.9 bitcast_add_fusion.1
  386.9 0.7 copy.73
  387.6 1.5 fusion.9
  389.1 12.7 %cholesky.55 = f32[128,128]{1,0:T(8,128)S(1)} custom-call(f32[128,128]{1,0:T(8,128)} %fusion.9), custom_call_target="Cholesky" | custom-call | tf_op jit(solution)/shard_map/jit(cholesky)/cholesky | solution.py:168
  401.9 0.6 copy-done.4
  402.4 0.6 compare_reduce_fusion
  403.1 2.0 select_bitcast_fusion
  405.1 11.3 %custom-call.7 = f32[1,128,128]{1,2,0:T(8,128)} custom-call(f32[1,128,128]{2,1,0:T(8,128)} %get-tuple-element.11), custom_call_target="InvertDiagBlocksLowerTriangular" | custom-call | tf_op jit(solution)/shard_map/triangular_solve/custom-call.0 | solution.py:169
  416.4 1.1 bitcast_dynamic-update-slice_fusion.1
  417.5 0.8 slice_dynamic-update-slice_fusion.small_ref
  418.3 1.7 convolution_select_fusion.1
  420.1 1.1 pad_maximum_fusion.1
  421.2 0.8 constant_dynamic-slice_fusion
  422.1 2.0 fusion
  424.1 20.6 %finish.1 = f32[24,512,128]{2,1,0:T(8,128)} custom-call(s32[48]{0:T(128)} %reshape.252.where, s32[3]{0:T(128)} %pad_add_fusion.place, f32[24,512,128]{2,1,0:T(8,128)} %bitcast.89, f32[24,128,128]{2,1,0:T(8,128)} %get-tuple-element.18.zero_ref, f32[24,128,128]{2,1,0:T(8,128)} %get-tuple-element.17.one_ref, f32[5,128,128]{2,1,0:T(8,128)} %copy-done.3, ...), custom_call_target="tpu_custom_call" | custom-call | tf_op jit(solution)/shard_map/finish/pallas_call | solution.py:146
  (40 shorter events, 1.7 us)
Async XLA Ops:
  6.5 134.1 %all-gather.6.cloned.1.call-start = ((), (), s32[]{:S(2)}) async-start(), calls=%async_computation.2 | async-start | bytes 9437184 | tf_op jit(solution)/shard_map/all_gather | solution.py:222
  188.6 93.8 %all-to-all-start = ((f16[16,2,128,512]{3,2,1,0:T(8,128)(2,1)}), f16[16,2,128,512]{3,2,1,0:T(8,128)(2,1)}, u32[]{:S(2)}, u32[]{:S(2)}) async-start(f16[16,2,128,512]{3,2,1,0:T(8,128)(2,1)} %bitcast.90), calls=%async_computation | async-start | bytes 8388608 | tf_op jit(solution)/shard_map/all_to_all | solution.py:224
  193.2 161.9 %all-gather.4.cloned.1.call-start = ((), (), s32[]{:S(2)}) async-start(), calls=%async_computation.1 | async-start | bytes 1114112 | tf_op jit(solution)/shard_map/all_gather | solution.py:234
  298.8 17.9 %collective-permute-start = (f16[24,128,128]{2,1,0:T(8,128)(2,1)S(1)}, f16[24,128,128]{2,1,0:T(8,128)(2,1)S(1)}, u32[]{:S(2)}, u32[]{:S(2)}) collective-permute-start(f16[24,128,128]{2,1,0:T(8,128)(2,1)S(1)} %convert_element_type.41), channel_id=1, source_target_pairs={{0,16},{16,0},{1,17},{17,1},{2,18},{18,2},{3,19},{19,3},{4,20},{20... | collective-permute-start | bytes 2359304 | tf_op jit(solution)/shard_map/ppermute | solution.py:236
  380.3 41.8 %copy-start = (f32[24,128,128]{2,1,0:T(8,128)S(1)}, f32[24,128,128]{2,1,0:T(8,128)}, u32[]{:S(2)}) copy-start(f32[24,128,128]{2,1,0:T(8,128)} %raw_column.1) | copy-start | bytes 4718596
  382.0 0.8 copy-start.1
  384.5 0.8 copy-start.2
  401.8 0.6 copy-start.4
  418.3 5.7 %copy-start.3 = (f32[5,128,128]{2,1,0:T(8,128)}, f32[5,128,128]{2,1,0:T(8,128)S(1)}, u32[]{:S(2)}) copy-start(f32[5,128,128]{2,1,0:T(8,128)S(1)} %slice_dynamic-update-slice_fusion.small_ref) | copy-start | bytes 983044
Sparse Core Ops, SparseCore 0:
  13.0 127.6 all-gather.5
  297.4 57.6 all-gather.3

commit v2 on v1

--- a/solution.py
+++ b/solution.py
@@ -9,6 +9,7 @@
 
 HIGHEST = lax.Precision.HIGHEST
 NT = (((1,), (1,)), ((), ()))
+PANELS = 2
 LINK = jnp.float16
 VMEM_LIMIT = 60 * 1024 * 1024
 
@@ -17,49 +18,64 @@
     return lax.dot_general(a, b, NT, precision=HIGHEST, preferred_element_type=jnp.float32)
 
 
-def contrib_kernel(half, slots, seats, factor_ref, update_ref, *rest):
+def contrib_kernel(group, half, slots, seats, factor_ref, update_ref, *rest):
     window_refs, out_ref, window = rest[: 2 * half], rest[2 * half], rest[2 * half + 1]
-
-    @pl.when(pl.program_id(0) == 0)
+    step = pl.program_id(0)
+
+    @pl.when(step == 0)
     def _():
         for p in range(2):
             for h in range(half):
                 window[p, h * 128 : (h + 1) * 128, :] = window_refs[2 * h + p][0]
 
+    pivots = factor_ref.shape[2]
+    rows = factor_ref[...].reshape(group * 128, pivots)
     for p in range(2):
-        product = lax.dot_general(
-            factor_ref[0], window[p], NT, preferred_element_type=jnp.float32
-        )
-        for h in range(half):
-            w = 2 * h + p
-            out_ref[p, 0, :, h * 128 : (h + 1) * 128] = (
-                update_ref[0, :, w * 128 : (w + 1) * 128] - product[:, h * 128 : (h + 1) * 128]
-            ).astype(out_ref.dtype)
-
-
-def contrib_blocks(factor, update, gathered, slots, seats, slot_count):
+        product = lax.dot_general(rows, window[p], NT, preferred_element_type=jnp.float32)
+        for g in range(group):
+            slot = slots[step * group + g]
+            for h in range(half):
+                w = 2 * h + p
+                out_ref[p, slot, :, h * 128 : (h + 1) * 128] = (
+                    update_ref[g, :, w * 128 : (w + 1) * 128]
+                    - product[g * 128 : (g + 1) * 128, h * 128 : (h + 1) * 128]
+                ).astype(out_ref.dtype)
+
+
+def contrib_blocks(factor, update, gathered, slots, seats, slot_count, group):
     rows, _, pivots = factor.shape
     cols = update.shape[2]
     half = cols // 256
+    once = pl.Buffered(1)
 
     def seat_map(w):
         return lambda i, slots, seats: (seats[w], 0, 0)
 
     return pl.pallas_call(
-        functools.partial(contrib_kernel, half),
+        functools.partial(contrib_kernel, group, half),
         out_shape=jax.ShapeDtypeStruct((2, slot_count, 128, half * 128), jnp.float32),
         grid_spec=pltpu.PrefetchScalarGridSpec(
             num_scalar_prefetch=2,
-            grid=(rows,),
+            grid=(rows // group,),
             in_specs=[
-                pl.BlockSpec((1, 128, pivots), lambda i, slots, seats: (i, 0, 0)),
-                pl.BlockSpec((1, 128, cols), lambda i, slots, seats: (i, 0, 0)),
+                pl.BlockSpec((group, 128, pivots), lambda i, slots, seats: (i, 0, 0)),
+                pl.BlockSpec((group, 128, cols), lambda i, slots, seats: (i, 0, 0)),
             ]
-            + [pl.BlockSpec((1, 128, pivots), seat_map(w)) for w in range(2 * half)],
+            + [
+                pl.BlockSpec((1, 128, pivots), seat_map(w), pipeline_mode=once)
+                for w in range(2 * half)
+            ],
             out_specs=pl.BlockSpec(
-                (2, 1, 128, half * 128), lambda i, slots, seats: (0, slots[i], 0, 0)
+                (2, slot_count, 128, half * 128),
+                lambda i, slots, seats: (0, 0, 0, 0),
+                pipeline_mode=once,
             ),
             scratch_shapes=[pltpu.VMEM((2, half * 128, pivots), jnp.bfloat16)],
+        ),
+        cost_estimate=pl.CostEstimate(
+            flops=2 * rows * 128 * cols * pivots,
+            bytes_accessed=rows * 128 * (2 * pivots + 6 * cols) + 2 * cols * pivots,
+            transcendentals=0,
         ),
         compiler_params=pltpu.CompilerParams(vmem_limit_bytes=VMEM_LIMIT),
         name="contrib",
@@ -194,11 +210,13 @@
 
     all_maps = child_map.reshape(pair_count, local_count, proc_count)
     child_maps = lax.dynamic_index_in_dim(all_maps, my_pair, 0, False)
-    lead_at = jnp.argmax((child_maps < proc_count).astype(jnp.int32), axis=0)
-    lead_ids = jnp.min(jnp.where(child_maps < proc_count, child_maps, proc_count), axis=0)
-    seats = jnp.argmax(
-        (lead_ids[None, :] == jnp.arange(block_cols)[:, None]).astype(jnp.int32), axis=1
+    inside = child_maps < proc_count
+    lead_at = jnp.argmax(inside.astype(jnp.int32), axis=0)
+    all_ids = jnp.min(jnp.where(all_maps < proc_count, all_maps, proc_count), axis=1)
+    all_seats = jnp.argmax(
+        (all_ids[:, None, :] == jnp.arange(proc_count)[None, :, None]).astype(jnp.int32), axis=2
     ).astype(jnp.int32)
+    seats = lax.dynamic_index_in_dim(all_seats, my_pair, 0, False)
     own_blocks = lax.dynamic_index_in_dim(child_maps, my_proc, 1, False)
     target = own_blocks % proc_count
     order = jnp.arange(local_count)
@@ -216,11 +234,19 @@
     where = jnp.max(jnp.where(match, source[..., None], -1), axis=(1, 2))
     where = where.reshape(pair_count * local_rows).astype(jnp.int32)
 
-    picked = lax.dynamic_index_in_dim(
-        factor, lax.dynamic_index_in_dim(lead_at, my_proc, 0, False), 0, True
-    )
+    my_lead = lax.dynamic_index_in_dim(lead_at, my_proc, 0, False)
+    picked = lax.dynamic_index_in_dim(factor, my_lead, 0, True)
     gathered = lax.all_gather(picked, "proc", axis=0, tiled=True)
-    packed = contrib_blocks(factor, update, gathered, slots, seats, slot_count)
+    ends = jnp.concatenate(
+        [lax.dynamic_index_in_dim(gathered, seats[k], 0, False) for k in range(PANELS)], axis=0
+    )
+    lead_part = lax.dynamic_slice(
+        update, (my_lead, 0, 0), (1, 128, PANELS * 128)
+    )[0] - lax.dot_general(picked[0], ends, NT, preferred_element_type=jnp.float32)
+    lead_sent = jnp.concatenate([lead_part, entries[0, ::half]], axis=1)
+    lead_all = lax.all_gather(lead_sent, ("pair", "proc"), axis=0, tiled=False)
+    lead_all = lead_all.reshape(2, proc_count, 128, (PANELS + 1) * 128)
+    packed = contrib_blocks(factor, update, gathered, slots, seats, slot_count, 4)
     arrived = lax.all_to_all(
         packed.astype(LINK).reshape(pair_count * proc_count, capacity, 128, half * 128),
         ("pair", "proc"),
@@ -230,16 +256,25 @@
     ).reshape(pair_count * slot_count, 128, half * 128)
     arrived = arrived.astype(jnp.float32)
 
+    shares = [
+        jnp.stack(
+            [lax.dynamic_index_in_dim(lead_all[c], all_seats[c, d], 0, False) for d in range(proc_count)]
+        )
+        for c in range(2)
+    ]
+    lead = jnp.stack(
+        [
+            lead_all[k, :, :, PANELS * 128 :]
+            + (shares[0] + shares[1])[:, :, k * 128 : (k + 1) * 128]
+            for k in range(PANELS)
+        ]
+    )
     column = raw_column(entries, arrived, where, 4)
-    lead = lax.all_gather(column[0], ("pair", "proc"), axis=0, tiled=False)
-    lead = lead.reshape(2, proc_count, 128, 128)
     other = lax.ppermute(column.astype(LINK), "pair", [(0, 1), (1, 0)]).astype(jnp.float32)
-    other_lead = lax.dynamic_index_in_dim(
-        lax.dynamic_index_in_dim(lead, 1 - my_pair, 0, False), my_proc, 0, True
-    )
-    other = jnp.concatenate([other_lead, other[1:]], axis=0)
-    zero = jnp.where(my_pair == 0, column, other)
-    one = jnp.where(my_pair == 0, other, column)
+    own_lead = lax.dynamic_index_in_dim(lead, my_proc, 1, False)
+    first_row = (jnp.arange(local_rows) == 0)[:, None, None]
+    zero = jnp.where(first_row, own_lead[0], jnp.where(my_pair == 0, column, other))
+    one = jnp.where(first_row, own_lead[1], jnp.where(my_pair == 0, other, column))
 
     ids = jnp.arange(block_cols)[:, None, None]
     pivot0, inverse0 = pivot_of(lead[0, 0])

time: 452 us -> 364 us (0.81)
  waiting for transfers between devices: 267 us -> 157 us
  between operations: 15.6 us -> 49.4 us
  Pallas kernels: 69.1 us -> 50.5 us
    all_to_all x1, waiting for transfers between devices: 88.3 us -> 12.4 us  [body(): lax.all_to_all(packed.astype(LINK).reshape(pair_count * proc_count, capac...]
    all_gather x1, waiting for transfers between devices: 38.3 us -> 5.09 us  [body(): lead_all = lax.all_gather(lead_sent, ('pair', 'proc'), axis=0, tiled=False)]
    pallas_call x1, Pallas kernels: 41.7 us -> 23.5 us  [contrib_blocks(): pl.pallas_call(functools.partial(contrib_kernel, group, half), out_shape=...]
  transfers between devices with their start and end apart: 4 -> 4, of which waited for: 4 -> 4; matrix products, arithmetic and copies ran while one was open for 1% -> 21% of each run, Pallas kernels for 0% -> 7%
where the time goes in v2:
time: 364 us; the launch traced here: 359 us
  waiting for transfers between devices  157 us (43%)
  other arithmetic  71.9 us (20%)
  Pallas kernels  50.5 us (14%)
  between operations  49.4 us (14%)
  local copies, waits for them, and re-layouts  16.8 us (5%)
  matrix products  8.15 us (2%)
  starting transfers between devices  5.75 us (2%)
    all_gather x1, waiting for transfers between devices, body(): gathered = lax.all_gather(picked, 'proc', axis=0, tiled=True)  122 us
    another operation x6, other arithmetic, pivot_of(): pivot = jnp.linalg.cholesky(jnp.tril(block) + jnp.tril(block, -1).T)  25 us
    pallas_call x1, Pallas kernels, contrib_blocks(): pl.pallas_call(functools.partial(contrib_kernel, group, half), out_shape=...  23.5 us
    another operation x4, other arithmetic, pivot_of(): lax.linalg.triangular_solve(pivot, jnp.eye(128, dtype=jnp.float32), left_...  21.5 us
    pallas_call x1, Pallas kernels, finish(): pl.pallas_call(functools.partial(finish_kernel, group, half), out_shape=j...  20.2 us
    ppermute x1, waiting for transfers between devices, body(): lax.ppermute(column.astype(LINK), 'pair', [(0, 1), (1, 0)])  17.3 us
    all_to_all x1, waiting for transfers between devices, body(): lax.all_to_all(packed.astype(LINK).reshape(pair_count * proc_count, capac...  12.4 us
  transfers between devices with their start and end apart: 4, of which 4 were waited for; matrix products, arithmetic and copies ran while one was open for 21% of the time, Pallas kernels for 7%

profile of v2, /device:TPU:0, one launch (start us, length us, event | category | flops | bytes accessed | tf_op | source)
XLA Modules:
  0.0 359.3 jit_solution(1398296768130837309)
XLA Ops:
  6.5 0.8 reshape.271
  7.4 0.6 bitcast_reduce_fusion
  8.0 0.6 dynamic_slice.90
  10.5 2.3 constant_dynamic-slice_fusion.2
  12.9 0.7 iota_reduce_fusion
  13.6 0.6 fusion.40
  16.6 1.0 slice.119
  18.8 121.9 %all-gather.5.cloned.1.call-done = bf16[8,1,1,128,4096]{4,3,2,1,0:T(8,128)(2,1)} async-done(((bf16[1,1,1,128,4096]{4,3,2,1,0:T(8,128)(2,1)}), bf16[8,1,1,128,4096]{4,3,2,1,0:T(8,128)(2,1)}) %all-gather.5.cloned.1.call-update) | async-done | bytes 8388624 | tf_op jit(solution)/shard_map/all_gather | solution.py:239
  140.7 1.7 dynamic-slice_bitcast_fusion.1
  142.3 2.1 fusion.6
  144.4 0.7 pad_maximum_fusion.1
  145.1 0.7 fusion.39
  166.2 0.6 fusion.43.seats
  167.5 23.5 %contrib.1 = f32[2,16,128,512]{3,2,1,0:T(8,128)} custom-call(s32[12]{0:T(128)} %multiply_add_fusion.slots, s32[8]{0:T(128)} %fusion.43.seats, bf16[12,128,4096]{2,1,0:T(8,128)(2,1)} %bitcast.144, f32[12,128,1024]{2,1,0:T(8,128)} %bitcast.148, bf16[8,128,4096]{2,1,0:T(8,128)(2,1)} %bitcast.132, bf16[8,128,4096]{2,1,0:T(8,128)(2,1)} %bitcast.133, ...), custom_call_target="tpu_custom_call" | custom-call | flops 12884901888 | bytes 30408704 | tf_op jit(solution)/shard_map/contrib/pallas_call | solution.py:54
  191.0 6.3 %convert_element_type.44 = f16[2,16,128,512]{3,2,1,0:T(8,128)(2,1)} convert(f32[2,16,128,512]{3,2,1,0:T(8,128)} %contrib.1) | non-fusion elementwise | flops 2097152 | bytes 12582912 | tf_op jit(solution)/shard_map/convert_element_type | solution.py:251
  197.3 4.7 %all-to-all-start = ((f16[16,2,128,512]{3,2,1,0:T(8,128)(2,1)}), f16[16,2,128,512]{3,2,1,0:T(8,128)(2,1)}, u32[]{:S(2)}, u32[]{:S(2)}) async-start(f16[16,2,128,512]{3,2,1,0:T(8,128)(2,1)} %bitcast.143), calls=%async_computation | async-start | bytes 8388608 | tf_op jit(solution)/shard_map/all_to_all | solution.py:250
  202.4 0.7 reshape.272.where
  214.1 0.7 pad_add_fusion.place
  214.8 0.6 iota_compare_fusion.9
  215.4 5.1 %all-gather.7.cloned.1.call-done = f32[2048,384]{1,0:T(8,128)} async-done(((f32[128,384]{1,0:T(8,128)}), f32[2048,384]{1,0:T(8,128)}) %all-gather.7.cloned.1.call-update) | async-done | bytes 3145744 | tf_op jit(solution)/shard_map/all_gather | solution.py:247
  220.4 2.1 fusion.38
  223.3 2.2 copy-done.1
  225.5 0.9 fusion.11
  226.4 0.8 copy-done.5
  227.3 0.9 bitcast_add_fusion.3
  228.4 11.7 %cholesky.44 = f32[128,128]{1,0:T(8,128)S(1)} custom-call(f32[128,128]{1,0:T(8,128)S(1)} %fusion.24), custom_call_target="Cholesky" | custom-call | tf_op jit(solution)/shard_map/jit(cholesky)/cholesky | solution.py:184
  240.1 0.7 compare_reduce_fusion.1
  240.8 0.7 select_bitcast_fusion.1
  241.5 10.4 %custom-call.6 = f32[1,128,128]{1,2,0:T(8,128)} custom-call(f32[1,128,128]{2,1,0:T(8,128)S(1)} %get-tuple-element.13), custom_call_target="InvertDiagBlocksLowerTriangular" | custom-call | tf_op jit(solution)/shard_map/triangular_solve/custom-call.0 | solution.py:185
  252.0 1.1 bitcast_dynamic-update-slice_fusion.3
  253.1 1.6 convolution_select_fusion.1
  254.8 1.8 convolution_subtract_fusion
  256.6 0.8 copy-done.7
  257.5 1.0 bitcast_add_fusion.1
  258.7 11.9 %cholesky.55 = f32[128,128]{1,0:T(8,128)S(1)} custom-call(f32[128,128]{1,0:T(8,128)S(1)} %fusion.20), custom_call_target="Cholesky" | custom-call | tf_op jit(solution)/shard_map/jit(cholesky)/cholesky | solution.py:184
  270.6 0.6 compare_reduce_fusion
  271.2 0.6 select_bitcast_fusion
  271.8 9.8 %custom-call.7 = f32[1,128,128]{1,2,0:T(8,128)S(1)} custom-call(f32[1,128,128]{2,1,0:T(8,128)S(1)} %get-tuple-element.11), custom_call_target="InvertDiagBlocksLowerTriangular" | custom-call | tf_op jit(solution)/shard_map/triangular_solve/custom-call.0 | solution.py:185
  281.9 1.2 convolution_select_fusion
  283.3 0.9 constant_dynamic-slice_fusion
  284.1 12.4 %all-to-all-done = f16[16,2,128,512]{3,2,1,0:T(8,128)(2,1)} async-done(((f16[16,2,128,512]{3,2,1,0:T(8,128)(2,1)}), f16[16,2,128,512]{3,2,1,0:T(8,128)(2,1)}, u32[]{:S(2)}, u32[]{:S(2)}) %all-to-all-start) | async-done | bytes 4194336 | tf_op jit(solution)/shard_map/all_to_all | solution.py:250
  296.6 6.5 %bitcast_convert_fusion.rest_0_.rest_1_.rest_2_.rest_3_.rest_4_.rest_5_.rest_6_.rest_7_ = f32[32,128,512]{2,1,0:T(8,128)} fusion(f16[16,2,128,512]{3,2,1,0:T(8,128)(2,1)} %all-to-all-done), kind=kLoop, calls=%fused_computation | loop fusion | flops 2097152 | bytes 12582912 | tf_op jit(solution)/shard_map/convert_element_type | solution.py:257
  303.1 6.9 %raw_column.1 = f32[24,128,128]{2,1,0:T(8,128)} custom-call(s32[48]{0:T(128)} %reshape.272.where, f32[24,512,128]{2,1,0:T(8,128)} %bitcast.141, f32[32,128,512]{2,1,0:T(8,128)} %bitcast_convert_fusion.rest_0_.rest_1_.rest_2_.rest_3_.rest_4_.rest_5_.rest_6_.rest_7_, ...), custom_call_target="tpu_custom_call" | custom-call | tf_op jit(solution)/shard_map/raw_column/pallas_call | solution.py:108
  310.0 1.7 convert_element_type.47
  311.7 1.0 collective-permute-start
  312.7 17.3 %collective-permute-done = f16[24,128,128]{2,1,0:T(8,128)(2,1)S(1)} collective-permute-done((f16[24,128,128]{2,1,0:T(8,128)(2,1)S(1)}, f16[24,128,128]{2,1,0:T(8,128)(2,1)S(1)}, u32[]{:S(2)}, u32[]{:S(2)}) %collective-permute-start) | collective-permute-done | bytes 786464 | tf_op jit(solution)/shard_map/ppermute | solution.py:273
  330.1 2.2 fusion.5
  332.4 20.2 %finish.1 = f32[24,512,128]{2,1,0:T(8,128)} custom-call(s32[48]{0:T(128)} %reshape.272.where, s32[3]{0:T(128)} %pad_add_fusion.place, f32[24,512,128]{2,1,0:T(8,128)} %bitcast.142, f32[24,128,128]{2,1,0:T(8,128)} %get-tuple-element.24.zero_ref, f32[24,128,128]{2,1,0:T(8,128)} %get-tuple-element.23.one_ref, f32[5,128,128]{2,1,0:T(8,128)} %copy-done.10, ...), custom_call_target="tpu_custom_call" | custom-call | tf_op jit(solution)/shard_map/finish/pallas_call | solution.py:162
  (79 shorter events, 4.1 us)
Async XLA Ops:
  6.5 134.1 %all-gather.5.cloned.1.call-start = ((), (), s32[]{:S(2)}) async-start(), calls=%async_computation.1 | async-start | bytes 9437184 | tf_op jit(solution)/shard_map/all_gather | solution.py:239
  12.9 207.6 %all-gather.7.cloned.1.call-start = ((), (), s32[]{:S(2)}) async-start(), calls=%async_computation.2 | async-start | bytes 3342336 | tf_op jit(solution)/shard_map/all_gather | solution.py:247
  197.3 99.2 %all-to-all-start = ((f16[16,2,128,512]{3,2,1,0:T(8,128)(2,1)}), f16[16,2,128,512]{3,2,1,0:T(8,128)(2,1)}, u32[]{:S(2)}, u32[]{:S(2)}) async-start(f16[16,2,128,512]{3,2,1,0:T(8,128)(2,1)} %bitcast.143), calls=%async_computation | async-start | bytes 8388608 | tf_op jit(solution)/shard_map/all_to_all | solution.py:250
  213.0 14.3 %copy-start.11 = (s32[128]{0:T(128)}, s32[128]{0:T(128)S(1)}, u32[]{:S(2)}) copy-start(s32[128]{0:T(128)S(1)} %iota_add_fusion) | copy-start | bytes 1540
  223.0 2.5 copy-start.1
  223.3 3.1 copy-start.2
  226.4 0.8 copy-start.5
  254.7 1.8 copy-start.3
  256.6 0.8 copy-start.7
  257.4 24.5 %copy-start.8 = (f32[8,128,128]{2,1,0:T(8,128)S(1)}, f32[8,128,128]{2,1,0:T(8,128)}, u32[]{:S(2)}) copy-start(f32[8,128,128]{2,1,0:T(8,128)} %copy-done.7) | copy-start | bytes 1572868
  257.4 25.8 %copy-start.4 = (f32[8,128,128]{2,1,0:T(8,128)S(1)}, f32[8,128,128]{2,1,0:T(8,128)}, u32[]{:S(2)}) copy-start(f32[8,128,128]{2,1,0:T(8,128)} %copy-done.3) | copy-start | bytes 1572868
  303.1 9.6 %copy-start.9 = (f32[1,8,128,128]{3,2,1,0:T(8,128)S(1)}, f32[1,8,128,128]{3,2,1,0:T(8,128)}, u32[]{:S(2)}) copy-start(f32[1,8,128,128]{3,2,1,0:T(8,128)} %get-tuple-element.19) | copy-start | bytes 1572868
  310.0 2.7 copy-start.6
  310.0 20.1 %copy-start = (f32[24,128,128]{2,1,0:T(8,128)S(1)}, f32[24,128,128]{2,1,0:T(8,128)}, u32[]{:S(2)}) copy-start(f32[24,128,128]{2,1,0:T(8,128)} %raw_column.1) | copy-start | bytes 4718596
  310.0 20.1 %copy-start.12 = (pred[24]{0:T(512)(128)(4,1)S(1)}, pred[24]{0:T(512)(128)(4,1)}, u32[]{:S(2)}) copy-start(pred[24]{0:T(512)(128)(4,1)} %iota_compare_fusion.12) | copy-start | bytes 76
  311.7 18.4 %collective-permute-start = (f16[24,128,128]{2,1,0:T(8,128)(2,1)S(1)}, f16[24,128,128]{2,1,0:T(8,128)(2,1)S(1)}, u32[]{:S(2)}, u32[]{:S(2)}) collective-permute-start(f16[24,128,128]{2,1,0:T(8,128)(2,1)S(1)} %convert_element_type.47), channel_id=1, source_target_pairs={{0,16},{16,0},{1,17},{17,1},{2,18},{18,2},{3,19},{19,3},{4,20},{20... | collective-permute-start | bytes 2359304 | tf_op jit(solution)/shard_map/ppermute | solution.py:273
  312.7 19.6 %copy-start.10 = (f32[5,128,128]{2,1,0:T(8,128)}, f32[5,128,128]{2,1,0:T(8,128)S(1)}, u32[]{:S(2)}) copy-start(f32[5,128,128]{2,1,0:T(8,128)S(1)} %slice_dynamic-update-slice_fusion.small_ref) | copy-start | bytes 983044
Sparse Core Ops, SparseCore 0:
  13.0 127.6 all-gather.4
  145.3 75.1 all-gather.6

commit v3 on v2

--- a/solution.py
+++ b/solution.py
@@ -14,8 +14,20 @@
 VMEM_LIMIT = 60 * 1024 * 1024
 
 
+def halves(x):
+    high = x.astype(jnp.bfloat16)
+    return high, (x - high.astype(jnp.float32)).astype(jnp.bfloat16)
+
+
 def nt_dot(a, b):
-    return lax.dot_general(a, b, NT, precision=HIGHEST, preferred_element_type=jnp.float32)
+    a_high, a_low = halves(a)
+    b_high, b_low = halves(b)
+    return lax.dot_general(
+        jnp.concatenate([a_high, a_high, a_low], axis=1),
+        jnp.concatenate([b_high, b_low, b_high], axis=1),
+        NT,
+        preferred_element_type=jnp.float32,
+    )
 
 
 def contrib_kernel(group, half, slots, seats, factor_ref, update_ref, *rest):
@@ -269,7 +281,7 @@
             for k in range(PANELS)
         ]
     )
-    column = raw_column(entries, arrived, where, 4)
+    column = raw_column(entries, arrived, where, 6)
     other = lax.ppermute(column.astype(LINK), "pair", [(0, 1), (1, 0)]).astype(jnp.float32)
     own_lead = lax.dynamic_index_in_dim(lead, my_proc, 1, False)
     first_row = (jnp.arange(local_rows) == 0)[:, None, None]

time: 364 us -> 357 us (0.981)
  Pallas kernels: 50.5 us -> 43.9 us
    pallas_call x1, Pallas kernels: 20.2 us -> 14 us  [finish(): pl.pallas_call(functools.partial(finish_kernel, group, half), out_shape=j...]
where the time goes in v3:
time: 357 us; the launch traced here: 353 us
  waiting for transfers between devices  157 us (44%)
  other arithmetic  71.9 us (20%)
  between operations  49.4 us (14%)
  Pallas kernels  43.9 us (12%)
  local copies, waits for them, and re-layouts  16.8 us (5%)
  matrix products  8.15 us (2%)
  starting transfers between devices  5.75 us (2%)
    all_gather x1, waiting for transfers between devices, body(): gathered = lax.all_gather(picked, 'proc', axis=0, tiled=True)  122 us
    another operation x6, other arithmetic, pivot_of(): pivot = jnp.linalg.cholesky(jnp.tril(block) + jnp.tril(block, -1).T)  25 us
    pallas_call x1, Pallas kernels, contrib_blocks(): pl.pallas_call(functools.partial(contrib_kernel, group, half), out_shape=...  23.5 us
    another operation x4, other arithmetic, pivot_of(): lax.linalg.triangular_solve(pivot, jnp.eye(128, dtype=jnp.float32), left_...  21.5 us
    ppermute x1, waiting for transfers between devices, body(): lax.ppermute(column.astype(LINK), 'pair', [(0, 1), (1, 0)])  17.6 us
    pallas_call x1, Pallas kernels, finish(): pl.pallas_call(functools.partial(finish_kernel, group, half), out_shape=j...  14 us
    all_to_all x1, waiting for transfers between devices, body(): lax.all_to_all(packed.astype(LINK).reshape(pair_count * proc_count, capac...  12.4 us
  transfers between devices with their start and end apart: 4, of which 4 were waited for; matrix products, arithmetic and copies ran while one was open for 21% of the time, Pallas kernels for 7%

profile of v3, /device:TPU:0, one launch (start us, length us, event | category | flops | bytes accessed | tf_op | source)
XLA Modules:
  0.0 353.0 jit_solution(6174165701422539264)
XLA Ops:
  6.5 0.8 reshape.271
  7.4 0.6 bitcast_reduce_fusion
  8.0 0.6 dynamic_slice.90
  10.5 2.3 constant_dynamic-slice_fusion.2
  12.9 0.7 iota_reduce_fusion
  13.6 0.6 fusion.40
  16.6 1.0 slice.119
  18.8 121.9 %all-gather.5.cloned.1.call-done = bf16[8,1,1,128,4096]{4,3,2,1,0:T(8,128)(2,1)} async-done(((bf16[1,1,1,128,4096]{4,3,2,1,0:T(8,128)(2,1)}), bf16[8,1,1,128,4096]{4,3,2,1,0:T(8,128)(2,1)}) %all-gather.5.cloned.1.call-update) | async-done | bytes 8388624 | tf_op jit(solution)/shard_map/all_gather | solution.py:251
  140.7 1.7 dynamic-slice_bitcast_fusion.1
  142.3 2.1 fusion.6
  144.4 0.7 pad_maximum_fusion.1
  145.1 0.7 fusion.39
  166.2 0.6 fusion.43.seats
  167.5 23.5 %contrib.1 = f32[2,16,128,512]{3,2,1,0:T(8,128)} custom-call(s32[12]{0:T(128)} %multiply_add_fusion.slots, s32[8]{0:T(128)} %fusion.43.seats, bf16[12,128,4096]{2,1,0:T(8,128)(2,1)} %bitcast.144, f32[12,128,1024]{2,1,0:T(8,128)} %bitcast.148, bf16[8,128,4096]{2,1,0:T(8,128)(2,1)} %bitcast.132, bf16[8,128,4096]{2,1,0:T(8,128)(2,1)} %bitcast.133, ...), custom_call_target="tpu_custom_call" | custom-call | flops 12884901888 | bytes 30408704 | tf_op jit(solution)/shard_map/contrib/pallas_call | solution.py:66
  191.0 6.3 %convert_element_type.44 = f16[2,16,128,512]{3,2,1,0:T(8,128)(2,1)} convert(f32[2,16,128,512]{3,2,1,0:T(8,128)} %contrib.1) | non-fusion elementwise | flops 2097152 | bytes 12582912 | tf_op jit(solution)/shard_map/convert_element_type | solution.py:263
  197.3 4.7 %all-to-all-start = ((f16[16,2,128,512]{3,2,1,0:T(8,128)(2,1)}), f16[16,2,128,512]{3,2,1,0:T(8,128)(2,1)}, u32[]{:S(2)}, u32[]{:S(2)}) async-start(f16[16,2,128,512]{3,2,1,0:T(8,128)(2,1)} %bitcast.143), calls=%async_computation | async-start | bytes 8388608 | tf_op jit(solution)/shard_map/all_to_all | solution.py:262
  202.4 0.7 reshape.272.where
  214.1 0.7 pad_add_fusion.place
  214.8 0.6 iota_compare_fusion.9
  215.4 5.1 %all-gather.7.cloned.1.call-done = f32[2048,384]{1,0:T(8,128)} async-done(((f32[128,384]{1,0:T(8,128)}), f32[2048,384]{1,0:T(8,128)}) %all-gather.7.cloned.1.call-update) | async-done | bytes 3145744 | tf_op jit(solution)/shard_map/all_gather | solution.py:259
  220.4 2.1 fusion.38
  223.3 2.2 copy-done.1
  225.5 0.9 fusion.11
  226.4 0.8 copy-done.5
  227.3 0.9 bitcast_add_fusion.3
  228.4 11.7 %cholesky.44 = f32[128,128]{1,0:T(8,128)S(1)} custom-call(f32[128,128]{1,0:T(8,128)S(1)} %fusion.24), custom_call_target="Cholesky" | custom-call | tf_op jit(solution)/shard_map/jit(cholesky)/cholesky | solution.py:196
  240.1 0.7 compare_reduce_fusion.1
  240.8 0.7 select_bitcast_fusion.1
  241.5 10.4 %custom-call.6 = f32[1,128,128]{1,2,0:T(8,128)} custom-call(f32[1,128,128]{2,1,0:T(8,128)S(1)} %get-tuple-element.13), custom_call_target="InvertDiagBlocksLowerTriangular" | custom-call | tf_op jit(solution)/shard_map/triangular_solve/custom-call.0 | solution.py:197
  252.0 1.1 bitcast_dynamic-update-slice_fusion.3
  253.1 1.6 convolution_select_fusion.1
  254.8 1.8 convolution_subtract_fusion
  256.6 0.8 copy-done.7
  257.5 1.0 bitcast_add_fusion.1
  258.7 11.9 %cholesky.55 = f32[128,128]{1,0:T(8,128)S(1)} custom-call(f32[128,128]{1,0:T(8,128)S(1)} %fusion.20), custom_call_target="Cholesky" | custom-call | tf_op jit(solution)/shard_map/jit(cholesky)/cholesky | solution.py:196
  270.6 0.6 compare_reduce_fusion
  271.2 0.6 select_bitcast_fusion
  271.8 9.8 %custom-call.7 = f32[1,128,128]{1,2,0:T(8,128)S(1)} custom-call(f32[1,128,128]{2,1,0:T(8,128)S(1)} %get-tuple-element.11), custom_call_target="InvertDiagBlocksLowerTriangular" | custom-call | tf_op jit(solution)/shard_map/triangular_solve/custom-call.0 | solution.py:197
  281.9 1.2 convolution_select_fusion
  283.3 0.9 constant_dynamic-slice_fusion
  284.1 12.4 %all-to-all-done = f16[16,2,128,512]{3,2,1,0:T(8,128)(2,1)} async-done(((f16[16,2,128,512]{3,2,1,0:T(8,128)(2,1)}), f16[16,2,128,512]{3,2,1,0:T(8,128)(2,1)}, u32[]{:S(2)}, u32[]{:S(2)}) %all-to-all-start) | async-done | bytes 4194336 | tf_op jit(solution)/shard_map/all_to_all | solution.py:262
  296.6 6.5 %bitcast_convert_fusion.rest_0_.rest_1_.rest_2_.rest_3_.rest_4_.rest_5_.rest_6_.rest_7_.rest_8_.rest_9_.rest_10_.rest_11_ = f32[32,128,512]{2,1,0:T(8,128)} fusion(f16[16,2,128,512]{3,2,1,0:T(8,128)(2,1)} %all-to-all-done), kind=kLoop, calls=%fused_computation | loop fusion | flops 2097152 | bytes 12582912 | tf_op jit(solution)/shard_map/convert_element_type | solution.py:269
  303.1 6.4 %raw_column.1 = f32[24,128,128]{2,1,0:T(8,128)} custom-call(s32[48]{0:T(128)} %reshape.272.where, f32[24,512,128]{2,1,0:T(8,128)} %bitcast.141, f32[32,128,512]{2,1,0:T(8,128)} %bitcast_convert_fusion.rest_0_.rest_1_.rest_2_.rest_3_.rest_4_.rest_5_.rest_6_.rest_7_.rest_8_.rest_9_.rest_10_.rest_11_, ...), custom_call_target="tpu_custom_call" | custom-call | tf_op jit(solution)/shard_map/raw_column/pallas_call | solution.py:120
  309.5 1.7 convert_element_type.47
  311.2 1.0 collective-permute-start
  312.3 17.6 %collective-permute-done = f16[24,128,128]{2,1,0:T(8,128)(2,1)S(1)} collective-permute-done((f16[24,128,128]{2,1,0:T(8,128)(2,1)S(1)}, f16[24,128,128]{2,1,0:T(8,128)(2,1)S(1)}, u32[]{:S(2)}, u32[]{:S(2)}) %collective-permute-start) | collective-permute-done | bytes 786464 | tf_op jit(solution)/shard_map/ppermute | solution.py:285
  329.9 2.2 fusion.5
  332.2 14.0 %finish.1 = f32[24,512,128]{2,1,0:T(8,128)} custom-call(s32[48]{0:T(128)} %reshape.272.where, s32[3]{0:T(128)} %pad_add_fusion.place, f32[24,512,128]{2,1,0:T(8,128)} %bitcast.142, f32[24,128,128]{2,1,0:T(8,128)} %get-tuple-element.24.zero_ref, f32[24,128,128]{2,1,0:T(8,128)} %get-tuple-element.23.one_ref, f32[5,128,128]{2,1,0:T(8,128)} %copy-done.10, ...), custom_call_target="tpu_custom_call" | custom-call | tf_op jit(solution)/shard_map/finish/pallas_call | solution.py:174
  (79 shorter events, 4.1 us)
Async XLA Ops:
  6.5 134.1 %all-gather.5.cloned.1.call-start = ((), (), s32[]{:S(2)}) async-start(), calls=%async_computation.1 | async-start | bytes 9437184 | tf_op jit(solution)/shard_map/all_gather | solution.py:251
  12.9 207.6 %all-gather.7.cloned.1.call-start = ((), (), s32[]{:S(2)}) async-start(), calls=%async_computation.2 | async-start | bytes 3342336 | tf_op jit(solution)/shard_map/all_gather | solution.py:259
  197.3 99.2 %all-to-all-start = ((f16[16,2,128,512]{3,2,1,0:T(8,128)(2,1)}), f16[16,2,128,512]{3,2,1,0:T(8,128)(2,1)}, u32[]{:S(2)}, u32[]{:S(2)}) async-start(f16[16,2,128,512]{3,2,1,0:T(8,128)(2,1)} %bitcast.143), calls=%async_computation | async-start | bytes 8388608 | tf_op jit(solution)/shard_map/all_to_all | solution.py:262
  213.0 14.3 %copy-start.11 = (s32[128]{0:T(128)}, s32[128]{0:T(128)S(1)}, u32[]{:S(2)}) copy-start(s32[128]{0:T(128)S(1)} %iota_add_fusion) | copy-start | bytes 1540
  223.0 2.5 copy-start.1
  223.3 3.1 copy-start.2
  226.4 0.8 copy-start.5
  254.7 1.8 copy-start.3
  256.6 0.8 copy-start.7
  257.4 24.5 %copy-start.8 = (f32[8,128,128]{2,1,0:T(8,128)S(1)}, f32[8,128,128]{2,1,0:T(8,128)}, u32[]{:S(2)}) copy-start(f32[8,128,128]{2,1,0:T(8,128)} %copy-done.7) | copy-start | bytes 1572868
  257.4 25.8 %copy-start.4 = (f32[8,128,128]{2,1,0:T(8,128)S(1)}, f32[8,128,128]{2,1,0:T(8,128)}, u32[]{:S(2)}) copy-start(f32[8,128,128]{2,1,0:T(8,128)} %copy-done.3) | copy-start | bytes 1572868
  303.1 9.1 %copy-start.9 = (f32[1,8,128,128]{3,2,1,0:T(8,128)S(1)}, f32[1,8,128,128]{3,2,1,0:T(8,128)}, u32[]{:S(2)}) copy-start(f32[1,8,128,128]{3,2,1,0:T(8,128)} %get-tuple-element.19) | copy-start | bytes 1572868
  309.5 2.7 copy-start.6
  309.5 20.4 %copy-start = (f32[24,128,128]{2,1,0:T(8,128)S(1)}, f32[24,128,128]{2,1,0:T(8,128)}, u32[]{:S(2)}) copy-start(f32[24,128,128]{2,1,0:T(8,128)} %raw_column.1) | copy-start | bytes 4718596
  309.5 20.4 %copy-start.12 = (pred[24]{0:T(512)(128)(4,1)S(1)}, pred[24]{0:T(512)(128)(4,1)}, u32[]{:S(2)}) copy-start(pred[24]{0:T(512)(128)(4,1)} %iota_compare_fusion.12) | copy-start | bytes 76
  311.2 18.7 %collective-permute-start = (f16[24,128,128]{2,1,0:T(8,128)(2,1)S(1)}, f16[24,128,128]{2,1,0:T(8,128)(2,1)S(1)}, u32[]{:S(2)}, u32[]{:S(2)}) collective-permute-start(f16[24,128,128]{2,1,0:T(8,128)(2,1)S(1)} %convert_element_type.47), channel_id=1, source_target_pairs={{0,16},{16,0},{1,17},{17,1},{2,18},{18,2},{3,19},{19,3},{4,20},{20... | collective-permute-start | bytes 2359304 | tf_op jit(solution)/shard_map/ppermute | solution.py:285
  312.3 19.9 %copy-start.10 = (f32[5,128,128]{2,1,0:T(8,128)}, f32[5,128,128]{2,1,0:T(8,128)S(1)}, u32[]{:S(2)}) copy-start(f32[5,128,128]{2,1,0:T(8,128)S(1)} %slice_dynamic-update-slice_fusion.small_ref) | copy-start | bytes 983044
Sparse Core Ops, SparseCore 0:
  13.0 127.6 all-gather.4
  145.3 75.1 all-gather.6
